TPU v7x, 1024 devices: a whole 8x8x8 slice. The times are simulated.
1024 devices in a mesh: brick: 64 (over x, y), row: 16 (over z, core).
Axes of the slice: x: 8, y: 8, z: 8, core: 2. Of those that a mesh axis runs over, the one named last changes fastest.
Arguments:
- flow_state: float32 [5, 256, 128, 128], P(None, 'brick', 'row'), may hold values from -1.2 to 3.5, as said below
- point_cell: int32 [16384, 64], P(('brick', 'row')), may hold values from 0 to 4095
- normals: float32 [3, 16384, 64], P(None, ('brick', 'row')), may hold values from -4 to 4
- rbf_weights: bfloat16 [16384, 64, 128], P(('brick', 'row')), may hold values from -0.75 to 0.75
- block_owner: int32 [16384, 1], P(('brick', 'row')), may hold values from 0 to 15; in each aligned block of 16 rows (0 to 15, 16 to 31, ...) at most 2 rows name the same one
- block_start: int32 [16384], P(('brick', 'row')), may hold values from 0 to 3968
- stiff_diag: float32 [128, 512], P('row'), may hold values from 0.05 to 0.5
- stiff_chord: float32 [128, 512], P('row'), may hold values from 0.3 to 3
Outputs:
- fluid_next: float32 [5, 256, 128, 128], P(None, 'brick', 'row')
- displacement: float32 [3, 128, 512], P(None, 'row')
- residual: float32 [3, 128, 512], P(None, 'row')
Inputs may be any that keep to these rules, and one draw needn't show every extreme that they name: `flow_state`: density (component 0) lies in 0.8 to 1.25, momenta in -1.2 to 1.2, energy in 1.6 to 3.5. `point_cell`: a cell of the device that holds the block. `block_owner`: of the 16 blocks of one device, at most 2 name the same owner. `block_start`: a node of the owner's 4096 nodes such that the window of 128 nodes stays within them.
All inputs are finite; a program needn't handle non-finite values.
Results may differ from a plain program's by a relative error of at most 0.003.
Values sent between devices are 32-bit elements; how exact they have to be, the bound alone decides.
A program may use at most 32 MiB of HBM per device.

v0:
```python
import jax
import jax.numpy as jnp
from jax import lax
from jax.sharding import PartitionSpec as P

ITERS = 3


GAMMA_LESS = 0.4
STEP_RATIO = 0.1
SMOOTHING = 0.1


def with_halo(block, sides, width, periodic):
    for axis, dim in sides:
        count = lax.axis_size(axis)
        forward = [(i, i + 1) for i in range(count - 1)]
        if periodic:
            forward.append((count - 1, 0))
        backward = [(target, source) for source, target in forward]
        low = lax.ppermute(
            lax.slice_in_dim(block, block.shape[dim] - width, None, axis=dim), axis, forward
        )
        high = lax.ppermute(lax.slice_in_dim(block, 0, width, axis=dim), axis, backward)
        block = jnp.concatenate([low, block, high], axis=dim)
    return block


def flux_along(state, direction):
    density = state[0]
    momenta = state[1:4]
    energy = state[4]
    velocity = momenta / density
    pressure = GAMMA_LESS * (energy - 0.5 * jnp.sum(momenta * velocity, axis=0))
    moving = velocity[direction]
    pieces = [momenta[direction]]
    for component in range(3):
        term = momenta[component] * moving
        if component == direction:
            term = term + pressure
        pieces.append(term)
    pieces.append((energy + pressure) * moving)
    return jnp.stack(pieces)


def pressure_of(state):
    density = state[0]
    momenta = state[1:4]
    energy = state[4]
    velocity = momenta / density
    return GAMMA_LESS * (energy - 0.5 * jnp.sum(momenta * velocity, axis=0))


def add_windows(total, forces, starts):
    window = forces.shape[2]

    def add_one(index, carry):
        start = starts[index]
        current = lax.dynamic_slice_in_dim(carry, start, window, 1)
        piece = lax.dynamic_index_in_dim(forces, index, 1, False)
        return lax.dynamic_update_slice_in_dim(carry, current + piece, start, 1)

    return lax.fori_loop(0, forces.shape[1], add_one, total)


def per_device(
    flow_state, point_cell, normals, rbf_weights, block_owner, block_start, stiff_diag, stiff_chord
):
    padded = with_halo(flow_state, (("brick", 1), ("row", 2)), 1, True)
    strip_first = padded[:, :, 1:-1, :]
    strip_second = padded[:, 1:-1, :, :]
    first_flux = flux_along(strip_first, 0)
    second_flux = flux_along(strip_second, 1)
    third_flux = flux_along(flow_state, 2)
    difference = (
        first_flux[:, 2:]
        - first_flux[:, :-2]
        + (second_flux[:, :, 2:] - second_flux[:, :, :-2])
        + (jnp.roll(third_flux, -1, 3) - jnp.roll(third_flux, 1, 3))
    )
    smoothed = (
        strip_first[:, 2:]
        + strip_first[:, :-2]
        + strip_second[:, :, 2:]
        + strip_second[:, :, :-2]
        + jnp.roll(flow_state, -1, 3)
        + jnp.roll(flow_state, 1, 3)
        - 6.0 * flow_state
    )
    fluid_next = flow_state - 0.5 * STEP_RATIO * difference + SMOOTHING * smoothed
    pressure = pressure_of(flow_state).reshape(-1)
    sampled = pressure[point_cell]
    traction = (sampled[None] * normals).astype(jnp.bfloat16)
    block_force = jnp.einsum(
        "cbp,bpw->cbw", traction, rbf_weights, preferred_element_type=jnp.float32
    )
    owners = lax.axis_size("row")
    span_rows = stiff_diag.shape[0]
    chord_count = stiff_diag.shape[1]
    span_nodes = span_rows * chord_count
    owner_row = block_owner[:, 0]
    flat_starts = owner_row * span_nodes + block_start
    spread_load = add_windows(
        jnp.zeros((3, owners * span_nodes), jnp.float32), block_force, flat_starts
    )
    spread_load = spread_load.reshape(3, owners * span_rows, chord_count)
    owned_load = lax.psum_scatter(spread_load, "row", scatter_dimension=1, tiled=True)
    loads = lax.psum(owned_load, "brick")
    chord_before = jnp.roll(stiff_chord, 1, 1)
    displacement = jnp.zeros_like(loads)
    residual = loads

    def inner_sum(first, second):
        return lax.psum(jnp.sum(first * second), "row")

    direction = loads
    norm_now = inner_sum(residual, residual)
    for iteration in range(ITERS):
        widened = with_halo(direction, (("row", 1),), 1, False)
        span_term = 2.0 * direction - widened[:, 2:] - widened[:, :-2]
        chord_term = stiff_chord * (direction - jnp.roll(direction, -1, 2)) + chord_before * (
            direction - jnp.roll(direction, 1, 2)
        )
        image = stiff_diag * direction + chord_term + span_term
        step_length = norm_now / inner_sum(direction, image)
        displacement = displacement + step_length * direction
        residual = residual - step_length * image
        norm_next = inner_sum(residual, residual)
        direction = residual + norm_next / norm_now * direction
        norm_now = norm_next
    return (fluid_next, displacement, residual)


def solution(mesh):
    return jax.shard_map(
        per_device,
        mesh=mesh,
        in_specs=(
            P(None, "brick", "row", None),
            P(("brick", "row"), None),
            P(None, ("brick", "row"), None),
            P(("brick", "row"), None, None),
            P(("brick", "row"), None),
            P(("brick", "row")),
            P("row", None),
            P("row", None),
        ),
        out_specs=(P(None, "brick", "row", None), P(None, "row", None), P(None, "row", None)),
        check_vma=False,
    )
```

profile of v0, /device:TPU:1, one launch (start us, length us, event | category | flops | bytes accessed | tf_op | source)
XLA Modules:
  0.0 587.6 jit_solution(16375532553536993028)
XLA Ops:
  7.2 0.8 fusion.46
  8.0 4.1 collective-permute-start
  12.2 6.8 %collective-permute-start.1 = (f32[5,1,8,128]{3,2,1,0:T(8,128)S(1)}, f32[5,1,8,128]{3,2,1,0:T(8,128)S(1)}, u32[]{:S(2)}, u32[]{:S(2)}) collective-permute-start(f32[5,1,8,128]{3,2,1,0:T(8,128)S(1)} %get-tuple-element.127), channel_id=1, source_target_pairs={{16,0},{32,16},{48,32},{64,48},{80,64},{96,80},{112,96},{128,112},... | collective-permute-start | bytes 61448 | tf_op jit(solution)/shard_map/ppermute | solution.py:24
  19.0 0.7 copy-done.5
  19.8 6.1 %gather_fusion = f32[1024]{0:T(1024)S(1)} fusion(f32[4096]{0:T(1024)S(1)} %fusion.35, s32[1024]{0:T(1024)S(1)} %broadcast_clamp_fusion), kind=kCustom, calls=%fused_computation | custom fusion | bytes 12288 | tf_op jit(solution)/shard_map/gather | solution.py:92
  27.0 45.2 %while.13 = (s32[]{:T(128)}, f32[3,65536]{1,0:T(4,128)S(1)}, s32[16]{0:T(128)S(1)}, f32[3,16,128]{2,0,1:T(4,128)S(1)}, s32[]{:T(128)}, /*index=5*/s32[]{:T(128)}, s32[]{:T(128)}) while((s32[]{:T(128)}, f32[3,65536]{1,0:T(4,128)S(1)}, s32[16]{0:T(128)S(1)}, f32[3,16,128]{2,0,1:T(4,128)S(1)}, s32[]{:T(128)}, /*index=5*/s32[]{:T(128)}, ...), condition=%wide.region_4.5_spmd, body=%wide.region_3.4_spmd.sunk | while | flops 389 | bytes 7823 | solution.py:63
  29.8 0.6 dynamic_slice.29
  32.6 0.6 dynamic_slice.29
  35.5 0.6 dynamic_slice.29
  38.3 0.6 dynamic_slice.29
  41.1 0.6 dynamic_slice.29
  43.9 0.6 dynamic_slice.29
  46.8 0.6 dynamic_slice.29
  49.6 0.6 dynamic_slice.29
  52.4 0.6 dynamic_slice.29
  55.2 0.6 dynamic_slice.29
  58.0 0.6 dynamic_slice.29
  60.9 0.6 dynamic_slice.29
  63.7 0.6 dynamic_slice.29
  66.5 0.6 dynamic_slice.29
  69.3 0.6 dynamic_slice.29
  72.2 1.1 copy.17
  73.6 0.6 copy-done.2
  74.4 3.8 collective-permute-start.2
  78.2 8.5 %collective-permute-start.3 = (f32[5,6,1,128]{3,2,1,0:T(1,128)S(1)}, f32[5,6,1,128]{3,2,1,0:T(1,128)S(1)}, u32[]{:S(2)}, u32[]{:S(2)}) collective-permute-start(f32[5,6,1,128]{3,2,1,0:T(1,128)S(1)} %get-tuple-element.115), channel_id=1, source_target_pairs={{1,0},{2,1},{3,2},{4,3},{5,4},{6,5},{7,6},{8,7},{9,8},{10,9},{11,1... | collective-permute-start | bytes 46088 | tf_op jit(solution)/shard_map/ppermute | solution.py:24
  87.7 55.5 %reduce-scatter.2.cloned.1.call-done = f32[3,8,512]{2,1,0:T(8,128)} async-done(((f32[3,128,512]{2,1,0:T(8,128)}), f32[3,8,512]{2,1,0:T(8,128)}) %reduce-scatter.2.cloned.1.call-update) | async-done | bytes 49168 | tf_op jit(solution)/shard_map/reduce_scatter | solution.py:107
  143.3 224.2 %psum.49 = f32[3,8,512]{2,1,0:T(8,128)S(1)} all-reduce(f32[3,8,512]{2,1,0:T(8,128)} %reduce-scatter.2.cloned.1.call-done), channel_id=1, replica_groups=mesh['brick'=64,'row'=16] {'brick'}, use_global_device_ids=true, to_apply=%region_6.7 | all-reduce | flops 12288 | bytes 98304 | tf_op jit(solution)/shard_map/psum | solution.py:108
  367.5 58.4 %collective-permute-start.5 = (f32[3,1,512]{2,1,0:T(1,128)S(1)}, f32[3,1,512]{2,1,0:T(1,128)S(1)}, u32[]{:S(2)}, u32[]{:S(2)}) collective-permute-start(f32[3,1,512]{2,1,0:T(1,128)S(1)} %get-tuple-element.146), channel_id=1, source_target_pairs={{0,1},{1,2},{2,3},{3,4},{4,5},{5,6},{6,7},{7,8},{8,9},{9,10},{10,1... | collective-permute-start | bytes 18440 | tf_op jit(solution)/shard_map/ppermute | solution.py:21
  426.0 3.2 collective-permute-start.4
  429.3 1.7 collective-permute-done.4
  430.9 0.7 multiply_reduce_fusion.6
  431.6 22.9 %all-reduce = (f32[]{:T(128)}, f32[]{:T(128)}) all-reduce(f32[]{:T(128)} %get-tuple-element.84, f32[]{:T(128)} %get-tuple-element.83), channel_id=1, replica_groups=mesh['brick'=64,'row'=16] {'row'}, use_global_device_ids=true, to_apply=%region_8.9 | all-reduce | flops 2 | bytes 16 | tf_op jit(solution)/shard_map/psum | solution.py:114
  455.9 0.6 multiply_reduce_fusion.5
  456.5 0.8 fusion.5
  457.3 25.2 %psum.52 = f32[]{:T(128)} all-reduce(f32[]{:T(128)} %multiply_reduce_fusion.5), channel_id=1, replica_groups=mesh['brick'=64,'row'=16] {'row'}, use_global_device_ids=true, to_apply=%region_12.13 | all-reduce | flops 1 | bytes 8 | tf_op jit(solution)/shard_map/psum | solution.py:114
  484.0 1.9 collective-permute-start.7
  485.9 2.4 collective-permute-start.6
  488.4 2.5 collective-permute-done.6
  490.9 0.7 multiply_reduce_fusion.4
  491.6 23.8 %psum.53 = f32[]{:T(128)} all-reduce(f32[]{:T(128)} %get-tuple-element.99), channel_id=1, replica_groups=mesh['brick'=64,'row'=16] {'row'}, use_global_device_ids=true, to_apply=%region_14.15 | all-reduce | flops 1 | bytes 8 | tf_op jit(solution)/shard_map/psum | solution.py:114
  516.7 0.6 multiply_reduce_fusion.3
  517.3 25.1 %psum.54 = f32[]{:T(128)} all-reduce(f32[]{:T(128)} %get-tuple-element.97), channel_id=1, replica_groups=mesh['brick'=64,'row'=16] {'row'}, use_global_device_ids=true, to_apply=%region_16.17 | all-reduce | flops 1 | bytes 8 | tf_op jit(solution)/shard_map/psum | solution.py:114
  543.8 4.0 collective-permute-start.9
  547.9 1.9 collective-permute-start.8
  549.9 2.9 collective-permute-done.8
  552.8 0.7 multiply_reduce_fusion.2
  553.5 25.3 %psum.55 = f32[]{:T(128)} all-reduce(f32[]{:T(128)} %get-tuple-element.95), channel_id=1, replica_groups=mesh['brick'=64,'row'=16] {'row'}, use_global_device_ids=true, to_apply=%region_18.19 | all-reduce | flops 1 | bytes 8 | tf_op jit(solution)/shard_map/psum | solution.py:114
  580.1 0.7 multiply_subtract_fusion
  (103 shorter events, 8.3 us)
Async XLA Ops:
  7.2 19.5 %copy-start = (bf16[16,64,128]{2,1,0:T(8,128)(2,1)S(1)}, bf16[16,64,128]{2,1,0:T(8,128)(2,1)}, u32[]{:S(2)}) copy-start(bf16[16,64,128]{2,1,0:T(8,128)(2,1)} %param.13) | copy-start | bytes 786436
  7.2 11.8 %copy-start.1 = (f32[5,4,8,128]{3,2,1,0:T(8,128)S(1)}, f32[5,4,8,128]{3,2,1,0:T(8,128)}, u32[]{:S(2)}) copy-start(f32[5,4,8,128]{3,2,1,0:T(8,128)} %param.10) | copy-start | bytes 245764
  7.2 136.1 %reduce-scatter.2.cloned.1.call-start = ((), (), s32[]{:S(2)}) async-start(), calls=%async_computation.1 | async-start | bytes 835584 | tf_op jit(solution)/shard_map/reduce_scatter | solution.py:107
  8.0 66.3 %collective-permute-start = (f32[5,1,8,128]{3,2,1,0:T(8,128)S(1)}, f32[5,1,8,128]{3,2,1,0:T(8,128)S(1)}, u32[]{:S(2)}, u32[]{:S(2)}) collective-permute-start(f32[5,1,8,128]{3,2,1,0:T(8,128)S(1)} %get-tuple-element.128), channel_id=1, source_target_pairs={{0,16},{16,32},{32,48},{48,64},{64,80},{80,96},{96,112},{112,128},... | collective-permute-start | bytes 61448 | tf_op jit(solution)/shard_map/ppermute | solution.py:21
  12.2 62.2 %collective-permute-start.1 = (f32[5,1,8,128]{3,2,1,0:T(8,128)S(1)}, f32[5,1,8,128]{3,2,1,0:T(8,128)S(1)}, u32[]{:S(2)}, u32[]{:S(2)}) collective-permute-start(f32[5,1,8,128]{3,2,1,0:T(8,128)S(1)} %get-tuple-element.127), channel_id=1, source_target_pairs={{16,0},{32,16},{48,32},{64,48},{80,64},{96,80},{112,96},{128,112},... | collective-permute-start | bytes 61448 | tf_op jit(solution)/shard_map/ppermute | solution.py:24
  19.0 0.7 copy-start.5
  19.8 6.8 %copy-start.4 = (f32[3,16,64]{2,1,0:T(8,128)S(1)}, f32[3,16,64]{2,1,0:T(8,128)}, u32[]{:S(2)}) copy-start(f32[3,16,64]{2,1,0:T(8,128)} %param.12) | copy-start | bytes 36868
  26.0 0.7 copy-start.6
  26.0 0.7 copy-start.7
  73.5 0.7 copy-start.2
  74.4 12.9 %collective-permute-start.2 = (f32[5,6,1,128]{3,2,1,0:T(1,128)S(1)}, f32[5,6,1,128]{3,2,1,0:T(1,128)S(1)}, u32[]{:S(2)}, u32[]{:S(2)}) collective-permute-start(f32[5,6,1,128]{3,2,1,0:T(1,128)S(1)} %get-tuple-element.116), channel_id=1, source_target_pairs={{0,1},{1,2},{2,3},{3,4},{4,5},{5,6},{6,7},{7,8},{8,9},{9,10},{10,1... | collective-permute-start | bytes 46088 | tf_op jit(solution)/shard_map/ppermute | solution.py:21
  78.2 9.3 %collective-permute-start.3 = (f32[5,6,1,128]{3,2,1,0:T(1,128)S(1)}, f32[5,6,1,128]{3,2,1,0:T(1,128)S(1)}, u32[]{:S(2)}, u32[]{:S(2)}) collective-permute-start(f32[5,6,1,128]{3,2,1,0:T(1,128)S(1)} %get-tuple-element.115), channel_id=1, source_target_pairs={{1,0},{2,1},{3,2},{4,3},{5,4},{6,5},{7,6},{8,7},{9,8},{10,9},{11,1... | collective-permute-start | bytes 46088 | tf_op jit(solution)/shard_map/ppermute | solution.py:24
  367.5 61.7 %collective-permute-start.5 = (f32[3,1,512]{2,1,0:T(1,128)S(1)}, f32[3,1,512]{2,1,0:T(1,128)S(1)}, u32[]{:S(2)}, u32[]{:S(2)}) collective-permute-start(f32[3,1,512]{2,1,0:T(1,128)S(1)} %get-tuple-element.146), channel_id=1, source_target_pairs={{0,1},{1,2},{2,3},{3,4},{4,5},{5,6},{6,7},{7,8},{8,9},{9,10},{10,1... | collective-permute-start | bytes 18440 | tf_op jit(solution)/shard_map/ppermute | solution.py:21
  425.9 5.0 copy-start.3
  426.0 4.9 collective-permute-start.4
  484.0 4.4 collective-permute-start.7
  485.9 4.9 collective-permute-start.6
  543.8 6.0 %collective-permute-start.9 = (f32[3,1,512]{2,1,0:T(1,128)S(1)}, f32[3,1,512]{2,1,0:T(1,128)S(1)}, u32[]{:S(2)}, u32[]{:S(2)}) collective-permute-start(f32[3,1,512]{2,1,0:T(1,128)S(1)} %get-tuple-element.134), channel_id=1, source_target_pairs={{0,1},{1,2},{2,3},{3,4},{4,5},{5,6},{6,7},{7,8},{8,9},{9,10},{10,1... | collective-permute-start | bytes 18440 | tf_op jit(solution)/shard_map/ppermute | solution.py:21
  547.9 4.9 collective-permute-start.8
Sparse Core Ops, SparseCore 0:
  73.4 69.7 reduce-scatter.1
where the time goes:
time: 589 us; the launch traced here: 588 us
  blocking collectives  347 us (59%)
  starting transfers between devices  95.1 us (16%)
  waiting for transfers between devices  63.4 us (11%)
  loops' own time  31.1 us (5%)
  local copies, waits for them, and re-layouts  23.8 us (4%)
  between operations  21.1 us (4%)
  other arithmetic  6.46 us (1%)
    psum x1, blocking collectives, per_device(): loads = lax.psum(owned_load, 'brick')  224 us
    psum x5, blocking collectives, inner_sum(): return lax.psum(jnp.sum(first * second), 'row')  122 us
    ppermute x5, starting transfers between devices, with_halo(): lax.ppermute(lax.slice_in_dim(block, block.shape[dim] - width, None, axis...  72.2 us
    reduce_scatter x1, waiting for transfers between devices, per_device(): lax.psum_scatter(spread_load, 'row', scatter_dimension=1, tiled=True)  55.5 us
    another operation x1, loops' own time, add_windows(): return lax.fori_loop(0, forces.shape[1], add_one, total)  31.1 us
    ppermute x5, starting transfers between devices, with_halo(): lax.ppermute(lax.slice_in_dim(block, 0, width, axis=dim), axis, backward)  22.8 us
  transfers between devices with their start and end apart: 11, of which 6 were waited for; matrix products, arithmetic and copies ran while one was open for 4% of the time, Pallas kernels for 0%

commit v1 on v0

v1 whole, which is shorter than its diff:
```python
import jax
import jax.numpy as jnp
from jax import lax
from jax.experimental import pallas as pl
from jax.experimental.pallas import tpu as pltpu
from jax.sharding import PartitionSpec as P

NX = 8
NY = 8
NBRICK = NX * NY
NROW = 16
NBLK = 16
BP = 64
SPAN = 8
HALO = 3
ROWS = SPAN + 2 * HALO
CENTRE = 4.0
WIDTH = 4.0
PRESSURE = 0.4
FLUX = 0.05
SMOOTH = 0.1
MESH = pl.DeviceIdType.MESH
F32 = jnp.float32
BF16 = jnp.bfloat16


def iota(shape, axis):
    return lax.broadcasted_iota(jnp.int32, shape, axis)


def three_terms(value):
    first = value.astype(BF16)
    rest = value - first.astype(F32)
    second = rest.astype(BF16)
    third = (rest - second.astype(F32)).astype(BF16)
    return first, second, third


def select_rows(chosen, values):
    chosen = chosen.astype(F32).astype(BF16)
    parts = [jnp.dot(chosen, term, preferred_element_type=F32) for term in three_terms(values)]
    return parts[0] + (parts[1] + parts[2])


def take_lanes(values, index):
    return jnp.take_along_axis(values, index, axis=1, mode="promise_in_bounds")


def sample_pressure(flow, cell, packed_cell, pressure):
    density = flow[0:32, :]
    inverse = 1.0 / density
    kinetic = jnp.zeros_like(density)
    for c in range(3):
        momentum = flow[32 * (c + 1) : 32 * (c + 2), :]
        kinetic = kinetic + momentum * (momentum * inverse)
    pressure[...] = PRESSURE * (flow[128:160, :] - 0.5 * kinetic)
    packed_cell[:, 0:BP] = cell[0:8, :]
    packed_cell[:, BP:128] = cell[8:16, :]
    index = packed_cell[...]
    high = index >> 7
    low = index & 127
    sampled = jnp.zeros((8, 128), F32)
    for k in range(32):
        line = jnp.broadcast_to(pressure[k : k + 1, :], (8, 128))
        sampled = jnp.where(high == k, take_lanes(line, low), sampled)
    return jnp.concatenate([sampled, pltpu.roll(sampled, BP, 1)], axis=0)[:, 0:BP]


def pack_windows(sampled, normals, weights, owner, start, send):
    traction = jnp.concatenate([(sampled * normals[c]).astype(BF16) for c in range(3)], axis=0)
    block_of_row = iota((48, 128), 0) & 15
    forces = jnp.zeros((48, 128), F32)
    for b in range(NBLK):
        product = jnp.dot(traction, weights[b], preferred_element_type=F32)
        forces = jnp.where(block_of_row == b, product, forces)
    block = (iota((16, 128), 1) & 15).astype(F32)
    named = jnp.broadcast_to(owner[...], (16, 128))
    begins = jnp.broadcast_to(start[...], (16, 128)).astype(F32)
    mine = named == iota((16, 128), 0)
    first = jnp.min(jnp.where(mine, block, 999.0), axis=1, keepdims=True)
    is_first = jnp.where(mine & (block == first), 1.0, 0.0)
    is_first = jnp.sum(is_first, axis=0, keepdims=True)
    key = 2.0 * named[0:1, :].astype(F32) + (1.0 - is_first)
    key = jnp.broadcast_to(key, (128, 128))
    row = iota((128, 128), 0)
    lane = iota((128, 128), 1)
    wanted = (2 * (row >> 3) + (row & 1)).astype(F32)
    match = key == wanted
    begin = jnp.sum(
        jnp.where(match, jnp.broadcast_to(begins[0:1, :], (128, 128)), 0.0), axis=1, keepdims=True
    )
    begin = jnp.broadcast_to(begin, (128, 128))
    chosen = match & ((lane >> 4) == ((row & 7) >> 1))
    windows = select_rows(chosen[:, 0:48], forces)
    shift = begin.astype(jnp.int32) & 127
    index = (lane - shift) & 127
    for o in range(NROW):
        part = slice(8 * o, 8 * o + 8)
        turned = take_lanes(windows[part], index[part])
        send[o] = jnp.where((row[part] & 7) < 6, turned, begin[part])


def add_windows(received, dense):
    values = received[...].reshape(128, 128)
    low = jnp.broadcast_to(received[:, 6:7, :], (16, 8, 128)).reshape(128, 128)
    high = jnp.broadcast_to(received[:, 7:8, :], (16, 8, 128)).reshape(128, 128)
    row = iota((128, 128), 0)
    lane = iota((128, 128), 1)
    begin = jnp.where((row & 1) == 0, low, high)
    shift = begin.astype(jnp.int32) & 127
    upright = jnp.sum(jnp.where(row == lane, begin, 0.0), axis=0, keepdims=True)
    line = jnp.broadcast_to(upright.astype(jnp.int32) >> 7, (128, 128))
    component = (lane & 7) >> 1
    fits = (component == ((row >> 2) & 3)) & (component < 3)
    place = 4 * (row >> 4) + (row & 3)
    window = (row & 7) < 6
    total = select_rows(fits & (place == line), jnp.where(window & (lane >= shift), values, 0.0))
    total = total + select_rows(fits & (place == line + 1), jnp.where(window & (lane < shift), values, 0.0))
    dense[...] = total.reshape(SPAN, 16, 128)


def turn(value, by, axis):
    size = value.shape[axis]
    return pltpu.roll(value, by % size, axis)


def next_node(value):
    turned = turn(value, -1, 1)
    sub = iota((8, 128), 0) & 3
    ahead = jnp.where(sub == 3, turn(turned, 3, 0), turn(turned, -1, 0))
    return jnp.where(iota((8, 128), 1) == 127, ahead, turned)


def node_before(value):
    turned = turn(value, 1, 1)
    sub = iota((8, 128), 0) & 3
    behind = jnp.where(sub == 0, turn(turned, -3, 0), turn(turned, 1, 0))
    return jnp.where(iota((8, 128), 1) == 0, behind, turned)


def pieces_along(state, direction):
    density, energy = state[0], state[4]
    inverse = 1.0 / density
    velocity = [state[1 + c] * inverse for c in range(3)]
    kinetic = state[1] * velocity[0] + state[2] * velocity[1] + state[3] * velocity[2]
    pressure = PRESSURE * (energy - 0.5 * kinetic)
    moving = velocity[direction]
    flux = [state[1 + direction]]
    for c in range(3):
        term = state[1 + c] * moving
        flux.append(term + pressure if c == direction else term)
    flux.append((energy + pressure) * moving)
    ahead = [SMOOTH * s + FLUX * f for s, f in zip(state, flux)]
    behind = [SMOOTH * s - FLUX * f for s, f in zip(state, flux)]
    return ahead, behind


def fluid_step(flow, x_low, x_high, y_low, y_high, result):
    own = [[flow[32 * f + 8 * i : 32 * f + 8 * i + 8, :] for f in range(5)] for i in range(4)]
    total = [[(1.0 - 6.0 * SMOOTH) * own[i][f] for f in range(5)] for i in range(4)]
    slab = [[x_low[f] for f in range(5)]] + own + [[x_high[f] for f in range(5)]]
    for i in range(6):
        ahead, behind = pieces_along(slab[i], 0)
        for f in range(5):
            if i <= 3:
                total[i][f] = total[i][f] + ahead[f]
            if i >= 2:
                total[i - 2][f] = total[i - 2][f] + behind[f]
    from_low, _ = pieces_along([y_low[4 * f : 4 * f + 4, :] for f in range(5)], 1)
    _, from_high = pieces_along([y_high[4 * f : 4 * f + 4, :] for f in range(5)], 1)
    sub = iota((8, 128), 0)
    for i in range(4):
        ahead, behind = pieces_along(own[i], 1)
        for f in range(5):
            low = jnp.broadcast_to(from_low[f][i : i + 1, :], (8, 128))
            high = jnp.broadcast_to(from_high[f][i : i + 1, :], (8, 128))
            total[i][f] = total[i][f] + jnp.where(sub == 0, low, turn(ahead[f], 1, 0))
            total[i][f] = total[i][f] + jnp.where(sub == 7, high, turn(behind[f], -1, 0))
        ahead, behind = pieces_along(own[i], 2)
        for f in range(5):
            total[i][f] = total[i][f] + turn(ahead[f], 1, 1) + turn(behind[f], -1, 1)
            result[32 * f + 8 * i : 32 * f + 8 * i + 8, :] = total[i][f]


def lay_stiffness(source, target):
    for s in range(SPAN):
        for j in range(4):
            line = source[s : s + 1, 128 * j : 128 * j + 128]
            target[s, j : j + 1, :] = line
            target[s, 4 + j : 5 + j, :] = line


def kernel(
    flow, cell, normals, weights, owner, start, stiff_diag, stiff_chord,
    fluid_next, displacement, residual,
    packed_cell, pressure, windows_out, windows_in, dense, x_in, x_sum, y_in, lines,
    shares_out, shares_in, y_edges, x_low, x_high, y_low, y_high,
    diag_rows, chord_rows, diag_halo, chord_halo, fields, turned,
    send_sem, recv_sem, fluid_send, fluid_recv, stiff_send, stiff_recv,
):
    brick = lax.axis_index("brick")
    row = lax.axis_index("row")
    x = lax.div(brick, NY)
    y = lax.rem(brick, NY)
    row_up = lax.rem(row + 1, NROW)
    row_down = lax.rem(row + NROW - 1, NROW)
    brick_up = lax.rem(brick + 1, NBRICK)
    brick_down = lax.rem(brick + NBRICK - 1, NBRICK)

    def x_peer(k):
        return lax.rem(x + k, NX) * NY + y

    def y_peer(k):
        return x * NY + lax.rem(y + k, NY)

    barrier = pltpu.get_barrier_semaphore()

    def greet(to_brick, to_row):
        pl.semaphore_signal(barrier, inc=1, device_id=(to_brick, to_row), device_id_type=MESH)

    @pl.loop(1, NROW)
    def _(k):
        greet(brick, lax.rem(row + k, NROW))

    @pl.loop(1, NX)
    def _(k):
        greet(x_peer(k), row)
        greet(x_peer(k), row_up)
        greet(x_peer(k), row_down)

    @pl.loop(1, NY)
    def _(k):
        greet(y_peer(k), row)

    greet(brick_up, row)
    greet(brick_down, row)

    def copy_to(source, target, send, receive, to_brick, to_row):
        return pltpu.make_async_remote_copy(
            src_ref=source, dst_ref=target, send_sem=send, recv_sem=receive,
            device_id=(to_brick, to_row), device_id_type=MESH,
        )

    sampled = sample_pressure(flow, cell, packed_cell, pressure)
    pack_windows(sampled, normals, weights, owner, start, windows_out)
    y_edges[...] = jnp.zeros((2, 24, 128), F32)
    y_edges[0, 0:20, :] = flow[pl.ds(0, 20, stride=8), :]
    y_edges[1, 0:20, :] = flow[pl.ds(7, 20, stride=8), :]

    pl.semaphore_wait(barrier, (NROW - 1) + 3 * (NX - 1) + (NY - 1) + 2)

    @pl.loop(1, NROW)
    def _(k):
        to = lax.rem(row + k, NROW)
        copy_to(windows_out.at[to], windows_in.at[row], send_sem.at[0], recv_sem.at[0], brick, to).start()

    windows_in[row] = windows_out[row]

    fluid_copies = [
        copy_to(y_edges.at[0], y_high, fluid_send.at[0], fluid_recv.at[0], brick, row_down),
        copy_to(y_edges.at[1], y_low, fluid_send.at[1], fluid_recv.at[1], brick, row_up),
    ]
    for f in range(5):
        plane = flow.at[pl.ds(32 * f, 8)]
        fluid_copies.append(
            copy_to(plane, x_high.at[f], fluid_send.at[2 + f], fluid_recv.at[2 + f], brick_down, row)
        )
        plane = flow.at[pl.ds(32 * f + 24, 8)]
        fluid_copies.append(
            copy_to(plane, x_low.at[f], fluid_send.at[7 + f], fluid_recv.at[7 + f], brick_up, row)
        )
    for copy in fluid_copies:
        copy.start()
    lay_stiffness(stiff_diag, diag_rows)
    lay_stiffness(stiff_chord, chord_rows)
    stiff_copies = []
    for n, (rows, halo) in enumerate(((diag_rows, diag_halo), (chord_rows, chord_halo))):
        stiff_copies.append(
            copy_to(rows.at[pl.ds(SPAN - 2, 2)], halo.at[0], stiff_send.at[2 * n], stiff_recv.at[2 * n], brick, row_up)
        )
        stiff_copies.append(
            copy_to(rows.at[pl.ds(0, 2)], halo.at[1], stiff_send.at[2 * n + 1], stiff_recv.at[2 * n + 1], brick, row_down)
        )
    for copy in stiff_copies:
        copy.start()

    def await_copies(buffer, count, n):
        part = buffer.at[pl.ds(0, count)]
        copy_to(part, part, send_sem.at[n], recv_sem.at[n], brick_up, row).wait_recv()

    await_copies(windows_in, NROW - 1, 0)
    add_windows(windows_in, dense)

    @pl.loop(1, NX)
    def _(k):
        to = lax.rem(x + k, NX)
        copy_to(dense.at[to], x_in.at[x], send_sem.at[1], recv_sem.at[1], x_peer(k), row).start()

    x_in[x] = dense[x]
    await_copies(x_in, NX - 1, 1)
    total = x_in[0]
    for k in range(1, NX):
        total = total + x_in[k]
    x_sum[...] = total

    @pl.loop(1, NY)
    def _(k):
        copy_to(x_sum, y_in.at[y], send_sem.at[2], recv_sem.at[2], y_peer(k), row).start()

    y_in[y] = total

    for copy in fluid_copies:
        copy.wait_recv()
    fluid_step(flow, x_low, x_high, y_low, y_high, fluid_next)
    for copy in stiff_copies:
        copy.wait_recv()

    await_copies(y_in, NY - 1, 2)
    total = y_in[0]
    for k in range(1, NY):
        total = total + y_in[k]
    lines[HALO + x] = total

    own_line = lines.at[HALO + x]

    @pl.loop(1, NX)
    def _(k):
        copy_to(own_line, own_line, send_sem.at[3], recv_sem.at[3], x_peer(k), row).start()

    goes_up = (x >= SPAN - HALO) & (row < NROW - 1)
    goes_down = (x < HALO) & (row > 0)

    @pl.when(goes_up)
    def _():
        @pl.loop(0, NX)
        def _(k):
            copy_to(own_line, lines.at[x - (SPAN - HALO)], send_sem.at[4], recv_sem.at[4], x_peer(k), row_up).start()

    @pl.when(goes_down)
    def _():
        @pl.loop(0, NX)
        def _(k):
            target = lines.at[HALO + SPAN + x]
            copy_to(own_line, target, send_sem.at[5], recv_sem.at[5], x_peer(k), row_down).start()

    @pl.when(row == 0)
    def _():
        lines[0:HALO] = jnp.zeros((HALO, 16, 128), F32)

    @pl.when(row == NROW - 1)
    def _():
        lines[HALO + SPAN : ROWS] = jnp.zeros((HALO, 16, 128), F32)

    await_copies(lines, NX - 1, 3)

    @pl.when(row > 0)
    def _():
        await_copies(lines, HALO, 4)

    @pl.when(row < NROW - 1)
    def _():
        await_copies(lines, HALO, 5)

    below = jnp.where(row > 0, 1.0, 0.0).astype(F32)
    above = jnp.where(row < NROW - 1, 1.0, 0.0).astype(F32)
    diag = [None, diag_halo[0, 0], diag_halo[0, 1]] + [diag_rows[s] for s in range(SPAN)]
    diag = diag + [diag_halo[1, 0], diag_halo[1, 1]]
    chord = [None, chord_halo[0, 0], chord_halo[0, 1]] + [chord_rows[s] for s in range(SPAN)]
    chord = chord + [chord_halo[1, 0], chord_halo[1, 1]]
    diag = [None if d is None else (d + (2.0 - CENTRE)) * (1.0 / WIDTH) for d in diag]
    chord = [None if d is None else d * (1.0 / WIDTH) for d in chord]
    products = [jnp.zeros((8, 128), F32) for _ in range(6)]
    for half in range(2):
        part = slice(8 * half, 8 * half + 8)
        levels = [[lines[i, part, :] for i in range(ROWS)]]
        for level in range(1, HALO + 1):
            before = levels[-1]
            after = [None] * ROWS
            for i in range(level, ROWS - level):
                flow_on = chord[i] * (before[i] - next_node(before[i]))
                value = diag[i] * before[i] + (flow_on - node_before(flow_on))
                value = value - (1.0 / WIDTH) * (before[i - 1] + before[i + 1])
                if i < HALO:
                    value = value * below
                if i >= HALO + SPAN:
                    value = value * above
                after[i] = value
            levels.append(after)
        for i in range(HALO, HALO + SPAN):
            for level in range(HALO + 1):
                fields[level, i - HALO, part, :] = levels[level][i]
            for n, (p, q) in enumerate(((0, 0), (0, 1), (1, 1), (1, 2), (2, 2), (2, 3))):
                products[n] = products[n] + levels[p][i] * levels[q][i]
    shares_out[...] = jnp.zeros((8, 128), F32)
    for n in range(6):
        shares_out[n : n + 1, :] = jnp.sum(products[n], axis=0, keepdims=True)

    @pl.loop(1, NROW)
    def _(k):
        to = lax.rem(row + k, NROW)
        copy_to(shares_out, shares_in.at[row], send_sem.at[6], recv_sem.at[6], brick, to).start()

    shares_in[row] = shares_out[...]

    for level in range(HALO + 1):
        for s in range(SPAN):
            for c in range(3):
                for j in range(4):
                    line = fields[level, s, 4 * c + j : 4 * c + j + 1, :]
                    turned[level, c, s : s + 1, 128 * j : 128 * j + 128] = line

    await_copies(shares_in, NROW - 1, 6)
    share = shares_in[0]
    for k in range(1, NROW):
        share = share + shares_in[k]
    share = jnp.broadcast_to(jnp.sum(share, axis=1, keepdims=True), (8, 128))
    moment = [jnp.broadcast_to(share[n : n + 1, :], (8, 128)) for n in range(6)]
    matrix = [CENTRE * moment[n] + WIDTH * moment[n + 1] for n in range(5)]
    m00, m01, m02, m11, m12, m22 = matrix[0], matrix[1], matrix[2], matrix[2], matrix[3], matrix[4]
    l10 = m01 / m00
    l20 = m02 / m00
    d1 = m11 - l10 * m01
    e = m12 - l10 * m02
    l21 = e / d1
    d2 = m22 - l20 * m02 - l21 * e
    y1 = moment[1] - l10 * moment[0]
    y2 = moment[2] - l20 * moment[0] - l21 * y1
    w2 = y2 / d2
    w1 = y1 / d1 - l21 * w2
    w0 = moment[0] / m00 - l10 * w1 - l20 * w2
    r0 = 1.0 - CENTRE * w0
    r1 = -(WIDTH * w0 + CENTRE * w1)
    r2 = -(WIDTH * w1 + CENTRE * w2)
    r3 = -(WIDTH * w2)
    for c in range(3):
        for j in range(4):
            part = slice(128 * j, 128 * j + 128)
            v = [turned[level, c, :, part] for level in range(4)]
            displacement[c, :, part] = w0 * v[0] + w1 * v[1] + w2 * v[2]
            residual[c, :, part] = (r0 * v[0] + r1 * v[1]) + (r2 * v[2] + r3 * v[3])

    def await_sent(buffer, count, n):
        part = buffer.at[pl.ds(0, count)]
        copy_to(part, part, send_sem.at[n], recv_sem.at[n], brick_up, row).wait_send()

    await_sent(windows_in, NROW - 1, 0)
    await_sent(x_in, NX - 1, 1)
    await_sent(y_in, NY - 1, 2)
    await_sent(lines, NX - 1, 3)

    @pl.when(goes_up)
    def _():
        await_sent(lines, NX, 4)

    @pl.when(goes_down)
    def _():
        await_sent(lines, NX, 5)

    await_sent(shares_in, NROW - 1, 6)
    for copy in fluid_copies + stiff_copies:
        copy.wait_send()


def per_device(
    flow_state, point_cell, normals, rbf_weights, block_owner, block_start, stiff_diag, stiff_chord
):
    flow = flow_state.reshape(160, 128)
    owner = jnp.tile(block_owner.reshape(1, NBLK), (1, 3))
    owner = jnp.pad(owner, ((0, 0), (0, 128 - 3 * NBLK)), constant_values=-1)
    start = jnp.pad(block_start.reshape(1, NBLK), ((0, 0), (0, 128 - NBLK)))
    vmem = pl.BlockSpec(memory_space=pltpu.VMEM)
    dma = pltpu.SemaphoreType.DMA
    fluid_next, displacement, residual = pl.pallas_call(
        kernel,
        out_shape=(
            jax.ShapeDtypeStruct((160, 128), F32),
            jax.ShapeDtypeStruct((3, SPAN, 512), F32),
            jax.ShapeDtypeStruct((3, SPAN, 512), F32),
        ),
        in_specs=[vmem] * 8,
        out_specs=(vmem, vmem, vmem),
        scratch_shapes=[
            pltpu.VMEM((8, 128), jnp.int32),
            pltpu.VMEM((32, 128), F32),
            pltpu.VMEM((NROW, 8, 128), F32),
            pltpu.VMEM((NROW, 8, 128), F32),
            pltpu.VMEM((SPAN, 16, 128), F32),
            pltpu.VMEM((NX, 16, 128), F32),
            pltpu.VMEM((16, 128), F32),
            pltpu.VMEM((NY, 16, 128), F32),
            pltpu.VMEM((ROWS, 16, 128), F32),
            pltpu.VMEM((8, 128), F32),
            pltpu.VMEM((NROW, 8, 128), F32),
            pltpu.VMEM((2, 24, 128), F32),
            pltpu.VMEM((5, 8, 128), F32),
            pltpu.VMEM((5, 8, 128), F32),
            pltpu.VMEM((24, 128), F32),
            pltpu.VMEM((24, 128), F32),
            pltpu.VMEM((SPAN, 8, 128), F32),
            pltpu.VMEM((SPAN, 8, 128), F32),
            pltpu.VMEM((2, 2, 8, 128), F32),
            pltpu.VMEM((2, 2, 8, 128), F32),
            pltpu.VMEM((HALO + 1, SPAN, 16, 128), F32),
            pltpu.VMEM((HALO + 1, 3, SPAN, 512), F32),
            dma((7,)),
            dma((7,)),
            dma((12,)),
            dma((12,)),
            dma((4,)),
            dma((4,)),
        ],
        compiler_params=pltpu.CompilerParams(
            collective_id=0, has_side_effects=True, vmem_limit_bytes=16 * 1024 * 1024
        ),
        cost_estimate=pl.CostEstimate(flops=20_000_000, bytes_accessed=600_000, transcendentals=0),
        name="coupling_step",
    )(flow, point_cell, normals, rbf_weights, owner, start, stiff_diag, stiff_chord)
    return fluid_next.reshape(5, 4, 8, 128), displacement, residual


def solution(mesh):
    return jax.shard_map(
        per_device,
        mesh=mesh,
        in_specs=(
            P(None, "brick", "row", None),
            P(("brick", "row"), None),
            P(None, ("brick", "row"), None),
            P(("brick", "row"), None, None),
            P(("brick", "row"), None),
            P(("brick", "row")),
            P("row", None),
            P("row", None),
        ),
        out_specs=(P(None, "brick", "row", None), P(None, "row", None), P(None, "row", None)),
        check_vma=False,
    )
```

time: 589 us -> 59.9 us (0.10)
  blocking collectives: 347 us -> 0 us
  starting transfers between devices: 95.1 us -> 0 us
  waiting for transfers between devices: 63.4 us -> 0 us
  Pallas kernels: 0 us -> 51.5 us
  loops' own time: 31.1 us -> 0 us
  between operations: 21.1 us -> 0.66 us
  local copies, waits for them, and re-layouts: 23.8 us -> 7.3 us
  other arithmetic: 6.46 us -> 0 us
    psum x6 -> x0, blocking collectives: 347 us -> none  [the longest x1 224 us: per_device(): loads = lax.psum(owned_load, 'brick')]
    ppermute x10 -> x0, starting transfers between devices: 95 us -> none  [the longest x5 72.2 us: with_halo(): lax.ppermute(lax.slice_in_dim(block, block.shape[dim] - width, None, axis...]
    reduce_scatter x1 -> x0, waiting for transfers between devices: 55.5 us -> none  [per_device(): lax.psum_scatter(spread_load, 'row', scatter_dimension=1, tiled=True)]
    pallas_call x0 -> x1, Pallas kernels: none -> 51.5 us  [per_device(): pl.pallas_call(kernel, out_shape=(jax.ShapeDtypeStruct((160, 128), F32),...]
    another operation x1 -> x0, loops' own time: 31.1 us -> none  [add_windows(): return lax.fori_loop(0, forces.shape[1], add_one, total)]
    dynamic_slice x16 -> x0, local copies, waits for them, and re-layouts: 9.44 us -> none  [add_one(): start = starts[index]]
    ppermute x10 -> x0, waiting for transfers between devices: 7.82 us -> none  [the longest x5 7.25 us: with_halo(): lax.ppermute(lax.slice_in_dim(block, 0, width, axis=dim), axis, backward)]
    gather x2 -> x0, local copies, waits for them, and re-layouts: 6.21 us -> none  [per_device(): sampled = pressure[point_cell]]
  transfers between devices with their start and end apart: 11 -> 0, of which waited for: 6 -> 0; matrix products, arithmetic and copies ran while one was open for 4% -> 0% of each run, Pallas kernels for 0% -> 0%
where the time goes in v1:
time: 59.9 us; the launch traced here: 59.4 us
  Pallas kernels  51.5 us (86%)
  local copies, waits for them, and re-layouts  7.3 us (12%)
  between operations  0.66 us (1%)
    pallas_call x1, Pallas kernels, per_device(): pl.pallas_call(kernel, out_shape=(jax.ShapeDtypeStruct((160, 128), F32),...  51.5 us
    unnamed x15, local copies, waits for them, and re-layouts  5.88 us

profile of v1, /device:TPU:1, one launch (start us, length us, event | category | flops | bytes accessed | tf_op | source)
XLA Modules:
  0.0 59.4 jit_solution(17622571458431312120)
XLA Ops:
  0.6 0.0 copy-start.5
  0.6 0.7 %pad.9.start = s32[1,128]{1,0:T(1,128)S(1)} pad(s32[1,16]{1,0:T(1,128)} %bitcast.7, s32[]{:T(128)} %constant.1.clone.1), padding=0_0x0_112 | pad | bytes 580 | tf_op jit(solution)/shard_map/jit(_pad)/pad | solution.py:470
  1.3 0.7 %tile.11 = s32[3,16]{1,0:T(4,128)S(1)} broadcast(s32[16]{0:T(128)} %bitcast.6), dimensions={1} | broadcast | bytes 256 | tf_op jit(solution)/shard_map/tile | solution.py:468
  2.0 0.1 tile.12
  2.1 0.0 copy-done.5
  2.1 0.0 copy-start
  2.1 0.9 %copy-done = bf16[16,64,128]{2,1,0:T(8,128)(2,1)S(1)} copy-done((bf16[16,64,128]{2,1,0:T(8,128)(2,1)S(1)}, bf16[16,64,128]{2,1,0:T(8,128)(2,1)}, u32[]{:S(2)}) %copy-start) | copy-done | bytes 262168
  3.0 0.0 copy-start.1
  3.0 0.9 %copy-done.1 = f32[5,4,8,128]{3,2,1,0:T(8,128)S(1)} copy-done((f32[5,4,8,128]{3,2,1,0:T(8,128)S(1)}, f32[5,4,8,128]{3,2,1,0:T(8,128)}, u32[]{:S(2)}) %copy-start.1) | copy-done | bytes 81944
  3.9 0.0 copy-start.2
  3.9 0.7 %copy-done.2 = f32[3,16,64]{2,1,0:T(8,128)S(1)} copy-done((f32[3,16,64]{2,1,0:T(8,128)S(1)}, f32[3,16,64]{2,1,0:T(8,128)}, u32[]{:S(2)}) %copy-start.2) | copy-done | bytes 12312
  4.6 0.0 copy-start.3
  4.6 0.7 %copy-done.3 = f32[8,512]{1,0:T(8,128)S(1)} copy-done((f32[8,512]{1,0:T(8,128)S(1)}, f32[8,512]{1,0:T(8,128)}, u32[]{:S(2)}) %copy-start.3) | copy-done | bytes 16408
  5.4 0.0 copy-start.4
  5.4 0.7 %copy-done.4 = f32[8,512]{1,0:T(8,128)S(1)} copy-done((f32[8,512]{1,0:T(8,128)S(1)}, f32[8,512]{1,0:T(8,128)}, u32[]{:S(2)}) %copy-start.4) | copy-done | bytes 16408
  6.1 51.5 %coupling_step.1 = (f32[160,128]{1,0:T(8,128)S(1)}, f32[3,8,512]{2,1,0:T(8,128)S(1)}, f32[3,8,512]{2,1,0:T(8,128)S(1)}) custom-call(f32[160,128]{1,0:T(8,128)S(1)} %bitcast.5, s32[16,64]{1,0:T(8,128)S(1)} %copy-done.5, f32[3,16,64]{2,1,0:T(8,128)S(1)} %copy-done.2, bf16[16,64,128]{2,1,0:T(8,128)(2,1)S(1)} %copy-done, s32[1,128]{1,0:T(1,128)S(1)} %pad.8.owner, ...), custom_call_target="tpu_custom_call" | custom-call | flops 20000000 | bytes 600000 | tf_op jit(solution)/shard_map/coupling_step/pallas_call | solution.py:473
  57.6 0.6 %copy.14 = f32[5,4,8,128]{3,2,1,0:T(8,128)} copy(f32[5,4,8,128]{3,2,1,0:T(8,128)S(1)} %bitcast.4) | data formatting | bytes 163840
  58.2 0.6 %copy.15 = f32[3,8,512]{2,1,0:T(8,128)} copy(f32[3,8,512]{2,1,0:T(8,128)S(1)} %get-tuple-element.13) | data formatting | bytes 98304
  58.8 0.6 %copy.16 = f32[3,8,512]{2,1,0:T(8,128)} copy(f32[3,8,512]{2,1,0:T(8,128)S(1)} %get-tuple-element.14) | data formatting | bytes 98304
  (1 shorter events, 0.0 us)
Async XLA Ops:
  0.6 1.4 %copy-start.5 = (s32[16,64]{1,0:T(8,128)S(1)}, s32[16,64]{1,0:T(8,128)}, u32[]{:S(2)}) copy-start(s32[16,64]{1,0:T(8,128)} %cell.1) | copy-start | bytes 12292
  2.1 1.0 %copy-start = (bf16[16,64,128]{2,1,0:T(8,128)(2,1)S(1)}, bf16[16,64,128]{2,1,0:T(8,128)(2,1)}, u32[]{:S(2)}) copy-start(bf16[16,64,128]{2,1,0:T(8,128)(2,1)} %weights.1) | copy-start | bytes 786436
  3.0 0.9 %copy-start.1 = (f32[5,4,8,128]{3,2,1,0:T(8,128)S(1)}, f32[5,4,8,128]{3,2,1,0:T(8,128)}, u32[]{:S(2)}) copy-start(f32[5,4,8,128]{3,2,1,0:T(8,128)} %param.8) | copy-start | bytes 245764
  3.9 0.7 %copy-start.2 = (f32[3,16,64]{2,1,0:T(8,128)S(1)}, f32[3,16,64]{2,1,0:T(8,128)}, u32[]{:S(2)}) copy-start(f32[3,16,64]{2,1,0:T(8,128)} %normals.1) | copy-start | bytes 36868
  4.6 0.7 %copy-start.3 = (f32[8,512]{1,0:T(8,128)S(1)}, f32[8,512]{1,0:T(8,128)}, u32[]{:S(2)}) copy-start(f32[8,512]{1,0:T(8,128)} %stiff_diag.1) | copy-start | bytes 49156
  5.4 0.7 %copy-start.4 = (f32[8,512]{1,0:T(8,128)S(1)}, f32[8,512]{1,0:T(8,128)}, u32[]{:S(2)}) copy-start(f32[8,512]{1,0:T(8,128)} %stiff_chord.1) | copy-start | bytes 49156

commit v2 on v1

--- a/solution.py
+++ b/solution.py
@@ -14,6 +14,9 @@
 SPAN = 8
 HALO = 3
 ROWS = SPAN + 2 * HALO
+LINE = 12
+FAR_FIRST = (4, 3, 5, 2, 6, 1, 7)
+ROW_FAR_FIRST = (8, 7, 9, 6, 10, 5, 11, 4, 12, 3, 13, 2, 14, 1, 15)
 CENTRE = 4.0
 WIDTH = 4.0
 PRESSURE = 0.4
@@ -28,18 +31,12 @@
     return lax.broadcasted_iota(jnp.int32, shape, axis)
 
 
-def three_terms(value):
-    first = value.astype(BF16)
-    rest = value - first.astype(F32)
-    second = rest.astype(BF16)
-    third = (rest - second.astype(F32)).astype(BF16)
-    return first, second, third
-
-
 def select_rows(chosen, values):
-    chosen = chosen.astype(F32).astype(BF16)
-    parts = [jnp.dot(chosen, term, preferred_element_type=F32) for term in three_terms(values)]
-    return parts[0] + (parts[1] + parts[2])
+    first = values.astype(BF16)
+    second = (values - first.astype(F32)).astype(BF16)
+    terms = jnp.concatenate([first, second], axis=1)
+    both = jnp.dot(chosen.astype(F32).astype(BF16), terms, preferred_element_type=F32)
+    return both[:, 0:128] + both[:, 128:256]
 
 
 def take_lanes(values, index):
@@ -63,41 +60,55 @@
     for k in range(32):
         line = jnp.broadcast_to(pressure[k : k + 1, :], (8, 128))
         sampled = jnp.where(high == k, take_lanes(line, low), sampled)
-    return jnp.concatenate([sampled, pltpu.roll(sampled, BP, 1)], axis=0)[:, 0:BP]
-
-
-def pack_windows(sampled, normals, weights, owner, start, send):
-    traction = jnp.concatenate([(sampled * normals[c]).astype(BF16) for c in range(3)], axis=0)
-    block_of_row = iota((48, 128), 0) & 15
-    forces = jnp.zeros((48, 128), F32)
-    for b in range(NBLK):
-        product = jnp.dot(traction, weights[b], preferred_element_type=F32)
-        forces = jnp.where(block_of_row == b, product, forces)
-    block = (iota((16, 128), 1) & 15).astype(F32)
-    named = jnp.broadcast_to(owner[...], (16, 128))
-    begins = jnp.broadcast_to(start[...], (16, 128)).astype(F32)
+    swapped = pltpu.roll(sampled, BP, 1)
+    left = iota((8, 128), 1) < BP
+    return jnp.concatenate(
+        [jnp.where(left, sampled, swapped), jnp.where(left, swapped, sampled)], axis=0
+    )
+
+
+def sort_blocks(owner, start, line_of):
+    line_of[0:1, :] = jnp.full((1, 128), -1, jnp.int32)
+    line_of[1:2, :] = jnp.zeros((1, 128), jnp.int32)
+    line_of[0:1, 0:NBLK] = owner[...]
+    line_of[1:2, 0:NBLK] = start[...]
+    lane = iota((16, 128), 1).astype(F32)
+    named = jnp.broadcast_to(line_of[0:1, :], (16, 128))
     mine = named == iota((16, 128), 0)
-    first = jnp.min(jnp.where(mine, block, 999.0), axis=1, keepdims=True)
-    is_first = jnp.where(mine & (block == first), 1.0, 0.0)
-    is_first = jnp.sum(is_first, axis=0, keepdims=True)
+    first = jnp.min(jnp.where(mine, lane, 999.0), axis=1, keepdims=True)
+    is_first = jnp.sum(jnp.where(mine & (lane == first), 1.0, 0.0), axis=0, keepdims=True)
     key = 2.0 * named[0:1, :].astype(F32) + (1.0 - is_first)
     key = jnp.broadcast_to(key, (128, 128))
+    begins = jnp.broadcast_to(line_of[1:2, :].astype(F32), (128, 128))
     row = iota((128, 128), 0)
-    lane = iota((128, 128), 1)
     wanted = (2 * (row >> 3) + (row & 1)).astype(F32)
-    match = key == wanted
-    begin = jnp.sum(
-        jnp.where(match, jnp.broadcast_to(begins[0:1, :], (128, 128)), 0.0), axis=1, keepdims=True
-    )
-    begin = jnp.broadcast_to(begin, (128, 128))
-    chosen = match & ((lane >> 4) == ((row & 7) >> 1))
-    windows = select_rows(chosen[:, 0:48], forces)
-    shift = begin.astype(jnp.int32) & 127
-    index = (lane - shift) & 127
+    begin = jnp.sum(jnp.where(key == wanted, begins, 0.0), axis=1, keepdims=True)
+    key = jnp.where(iota((128, 128), 1) < NBLK, key, -1.0)
+    again = jnp.maximum(key, jnp.maximum(shifted(key, 16), shifted(key, 32)))
+    component = iota((128, 128), 1) >> 4
+    chosen = (again == wanted) & (component == ((row & 7) >> 1))
+    return chosen[:, 0:48], jnp.broadcast_to(begin, (128, 128))
+
+
+def shifted(value, by):
+    return jnp.broadcast_to(pltpu.roll(value[0:8], by, 1)[0:1], value.shape)
+
+
+def pack_windows(sampled, normals, doubled, weights, chosen, begin, send):
+    doubled[:, :, 0:BP] = normals[...]
+    doubled[:, :, BP:128] = normals[...]
+    traction = jnp.concatenate([sampled * doubled[c] for c in range(3)], axis=0)
+    block = iota((48, 128), 0) & 15
+    half = iota((48, 128), 1) >> 6
+    spread = [jnp.where(block == 2 * g + half, traction, 0.0).astype(BF16) for g in range(8)]
+    forces = jnp.dot(jnp.concatenate(spread, axis=1), weights[...], preferred_element_type=F32)
+    windows = select_rows(chosen, forces)
+    index = (iota((128, 128), 1) - (begin.astype(jnp.int32) & 127)) & 127
+    sub = iota((8, 128), 0)
     for o in range(NROW):
         part = slice(8 * o, 8 * o + 8)
         turned = take_lanes(windows[part], index[part])
-        send[o] = jnp.where((row[part] & 7) < 6, turned, begin[part])
+        send[o] = jnp.where(sub < 6, turned, begin[part])
 
 
 def add_windows(received, dense):
@@ -114,9 +125,12 @@
     fits = (component == ((row >> 2) & 3)) & (component < 3)
     place = 4 * (row >> 4) + (row & 3)
     window = (row & 7) < 6
-    total = select_rows(fits & (place == line), jnp.where(window & (lane >= shift), values, 0.0))
-    total = total + select_rows(fits & (place == line + 1), jnp.where(window & (lane < shift), values, 0.0))
-    dense[...] = total.reshape(SPAN, 16, 128)
+    here = jnp.where(window & (lane >= shift), values, 0.0)
+    after = jnp.where(window & (lane < shift), values, 0.0)
+    chosen = jnp.concatenate([fits & (place == line), fits & (place == line + 1)], axis=1)
+    total = select_rows(chosen, jnp.concatenate([here, after], axis=0))
+    for s in range(SPAN):
+        dense[s] = total[16 * s : 16 * s + LINE]
 
 
 def turn(value, by, axis):
@@ -191,12 +205,13 @@
 
 
 def kernel(
+    flow_far, cell_far, normals_far, weights_far, owner_far, start_far, diag_far, chord_far,
+    fluid_next, displacement, residual,
     flow, cell, normals, weights, owner, start, stiff_diag, stiff_chord,
-    fluid_next, displacement, residual,
-    packed_cell, pressure, windows_out, windows_in, dense, x_in, x_sum, y_in, lines,
+    packed_cell, line_of, doubled, pressure, windows_out, windows_in, dense, x_in, x_sum, y_in, lines,
     shares_out, shares_in, y_edges, x_low, x_high, y_low, y_high,
     diag_rows, chord_rows, diag_halo, chord_halo, fields, turned,
-    send_sem, recv_sem, fluid_send, fluid_recv, stiff_send, stiff_recv,
+    load_sem, send_sem, recv_sem, fluid_send, fluid_recv, stiff_send, stiff_recv,
 ):
     brick = lax.axis_index("brick")
     row = lax.axis_index("row")
@@ -218,20 +233,25 @@
     def greet(to_brick, to_row):
         pl.semaphore_signal(barrier, inc=1, device_id=(to_brick, to_row), device_id_type=MESH)
 
-    @pl.loop(1, NROW)
-    def _(k):
+    for k in ROW_FAR_FIRST:
         greet(brick, lax.rem(row + k, NROW))
 
-    @pl.loop(1, NX)
-    def _(k):
+    loads = [
+        pltpu.make_async_copy(far, near, load_sem.at[n])
+        for n, (far, near) in enumerate((
+            (flow_far, flow), (cell_far, cell), (weights_far, weights), (normals_far, normals),
+            (owner_far, owner), (start_far, start), (diag_far, stiff_diag), (chord_far, stiff_chord),
+        ))
+    ]
+    for load in loads:
+        load.start()
+
+    for k in FAR_FIRST:
         greet(x_peer(k), row)
+        greet(y_peer(k), row)
+    for k in FAR_FIRST:
         greet(x_peer(k), row_up)
         greet(x_peer(k), row_down)
-
-    @pl.loop(1, NY)
-    def _(k):
-        greet(y_peer(k), row)
-
     greet(brick_up, row)
     greet(brick_down, row)
 
@@ -241,16 +261,22 @@
             device_id=(to_brick, to_row), device_id_type=MESH,
         )
 
+    loads[4].wait()
+    loads[5].wait()
+    chosen, begin = sort_blocks(owner, start, line_of)
+    loads[0].wait()
+    loads[1].wait()
     sampled = sample_pressure(flow, cell, packed_cell, pressure)
-    pack_windows(sampled, normals, weights, owner, start, windows_out)
+    loads[2].wait()
+    loads[3].wait()
+    pack_windows(sampled, normals, doubled, weights, chosen, begin, windows_out)
     y_edges[...] = jnp.zeros((2, 24, 128), F32)
     y_edges[0, 0:20, :] = flow[pl.ds(0, 20, stride=8), :]
     y_edges[1, 0:20, :] = flow[pl.ds(7, 20, stride=8), :]
 
     pl.semaphore_wait(barrier, (NROW - 1) + 3 * (NX - 1) + (NY - 1) + 2)
 
-    @pl.loop(1, NROW)
-    def _(k):
+    for k in ROW_FAR_FIRST:
         to = lax.rem(row + k, NROW)
         copy_to(windows_out.at[to], windows_in.at[row], send_sem.at[0], recv_sem.at[0], brick, to).start()
 
@@ -271,6 +297,8 @@
         )
     for copy in fluid_copies:
         copy.start()
+    loads[6].wait()
+    loads[7].wait()
     lay_stiffness(stiff_diag, diag_rows)
     lay_stiffness(stiff_chord, chord_rows)
     stiff_copies = []
@@ -291,8 +319,7 @@
     await_copies(windows_in, NROW - 1, 0)
     add_windows(windows_in, dense)
 
-    @pl.loop(1, NX)
-    def _(k):
+    for k in FAR_FIRST:
         to = lax.rem(x + k, NX)
         copy_to(dense.at[to], x_in.at[x], send_sem.at[1], recv_sem.at[1], x_peer(k), row).start()
 
@@ -303,8 +330,7 @@
         total = total + x_in[k]
     x_sum[...] = total
 
-    @pl.loop(1, NY)
-    def _(k):
+    for k in FAR_FIRST:
         copy_to(x_sum, y_in.at[y], send_sem.at[2], recv_sem.at[2], y_peer(k), row).start()
 
     y_in[y] = total
@@ -323,33 +349,34 @@
 
     own_line = lines.at[HALO + x]
 
-    @pl.loop(1, NX)
-    def _(k):
-        copy_to(own_line, own_line, send_sem.at[3], recv_sem.at[3], x_peer(k), row).start()
-
     goes_up = (x >= SPAN - HALO) & (row < NROW - 1)
     goes_down = (x < HALO) & (row > 0)
 
-    @pl.when(goes_up)
-    def _():
-        @pl.loop(0, NX)
-        def _(k):
-            copy_to(own_line, lines.at[x - (SPAN - HALO)], send_sem.at[4], recv_sem.at[4], x_peer(k), row_up).start()
-
-    @pl.when(goes_down)
-    def _():
-        @pl.loop(0, NX)
-        def _(k):
-            target = lines.at[HALO + SPAN + x]
-            copy_to(own_line, target, send_sem.at[5], recv_sem.at[5], x_peer(k), row_down).start()
+    def send_beside(steps):
+        @pl.when(goes_up)
+        def _():
+            for k in steps:
+                target = lines.at[x - (SPAN - HALO)]
+                copy_to(own_line, target, send_sem.at[4], recv_sem.at[4], x_peer(k), row_up).start()
+
+        @pl.when(goes_down)
+        def _():
+            for k in steps:
+                target = lines.at[HALO + SPAN + x]
+                copy_to(own_line, target, send_sem.at[5], recv_sem.at[5], x_peer(k), row_down).start()
+
+    send_beside((4, 3, 5))
+    for k in FAR_FIRST:
+        copy_to(own_line, own_line, send_sem.at[3], recv_sem.at[3], x_peer(k), row).start()
+    send_beside((2, 6, 1, 7, 0))
 
     @pl.when(row == 0)
     def _():
-        lines[0:HALO] = jnp.zeros((HALO, 16, 128), F32)
+        lines[0:HALO] = jnp.zeros((HALO, LINE, 128), F32)
 
     @pl.when(row == NROW - 1)
     def _():
-        lines[HALO + SPAN : ROWS] = jnp.zeros((HALO, 16, 128), F32)
+        lines[HALO + SPAN : ROWS] = jnp.zeros((HALO, LINE, 128), F32)
 
     await_copies(lines, NX - 1, 3)
 
@@ -372,7 +399,11 @@
     products = [jnp.zeros((8, 128), F32) for _ in range(6)]
     for half in range(2):
         part = slice(8 * half, 8 * half + 8)
-        levels = [[lines[i, part, :] for i in range(ROWS)]]
+        if half == 0:
+            levels = [[lines[i, 0:8, :] for i in range(ROWS)]]
+        else:
+            spare = jnp.zeros((4, 128), F32)
+            levels = [[jnp.concatenate([lines[i, 8:LINE, :], spare], axis=0) for i in range(ROWS)]]
         for level in range(1, HALO + 1):
             before = levels[-1]
             after = [None] * ROWS
@@ -391,12 +422,14 @@
                 fields[level, i - HALO, part, :] = levels[level][i]
             for n, (p, q) in enumerate(((0, 0), (0, 1), (1, 1), (1, 2), (2, 2), (2, 3))):
                 products[n] = products[n] + levels[p][i] * levels[q][i]
-    shares_out[...] = jnp.zeros((8, 128), F32)
+    share = jnp.zeros((1, 128), F32)
+    lane = iota((1, 128), 1)
     for n in range(6):
-        shares_out[n : n + 1, :] = jnp.sum(products[n], axis=0, keepdims=True)
-
-    @pl.loop(1, NROW)
-    def _(k):
+        inner = jnp.sum(jnp.sum(products[n], axis=0, keepdims=True), axis=1, keepdims=True)
+        share = jnp.where(lane == n, jnp.broadcast_to(inner, (1, 128)), share)
+    shares_out[...] = share
+
+    for k in ROW_FAR_FIRST:
         to = lax.rem(row + k, NROW)
         copy_to(shares_out, shares_in.at[row], send_sem.at[6], recv_sem.at[6], brick, to).start()
 
@@ -413,8 +446,7 @@
     share = shares_in[0]
     for k in range(1, NROW):
         share = share + shares_in[k]
-    share = jnp.broadcast_to(jnp.sum(share, axis=1, keepdims=True), (8, 128))
-    moment = [jnp.broadcast_to(share[n : n + 1, :], (8, 128)) for n in range(6)]
+    moment = [jnp.broadcast_to(share[:, n : n + 1], (8, 128)) for n in range(6)]
     matrix = [CENTRE * moment[n] + WIDTH * moment[n + 1] for n in range(5)]
     m00, m01, m02, m11, m12, m22 = matrix[0], matrix[1], matrix[2], matrix[2], matrix[3], matrix[4]
     l10 = m01 / m00
@@ -461,36 +493,62 @@
         copy.wait_send()
 
 
+def write_out(fluid, displacement, residual, fluid_far, displacement_far, residual_far, sem):
+    copies = [
+        pltpu.make_async_copy(near, far, sem.at[n])
+        for n, (near, far) in enumerate(
+            ((fluid, fluid_far), (displacement, displacement_far), (residual, residual_far))
+        )
+    ]
+    for copy in copies:
+        copy.start()
+    for copy in copies:
+        copy.wait()
+
+
 def per_device(
     flow_state, point_cell, normals, rbf_weights, block_owner, block_start, stiff_diag, stiff_chord
 ):
     flow = flow_state.reshape(160, 128)
-    owner = jnp.tile(block_owner.reshape(1, NBLK), (1, 3))
-    owner = jnp.pad(owner, ((0, 0), (0, 128 - 3 * NBLK)), constant_values=-1)
-    start = jnp.pad(block_start.reshape(1, NBLK), ((0, 0), (0, 128 - NBLK)))
+    weights = rbf_weights.reshape(NBLK * BP, 128)
+    owner = block_owner.reshape(1, NBLK)
+    start = block_start.reshape(1, NBLK)
+    arrays = (flow, point_cell, normals, weights, owner, start, stiff_diag, stiff_chord)
     vmem = pl.BlockSpec(memory_space=pltpu.VMEM)
+    far = pl.BlockSpec(memory_space=pltpu.HBM)
     dma = pltpu.SemaphoreType.DMA
-    fluid_next, displacement, residual = pl.pallas_call(
+    shapes = (
+        jax.ShapeDtypeStruct((160, 128), F32),
+        jax.ShapeDtypeStruct((3, SPAN, 512), F32),
+        jax.ShapeDtypeStruct((3, SPAN, 512), F32),
+    )
+    results = pl.pallas_call(
         kernel,
-        out_shape=(
-            jax.ShapeDtypeStruct((160, 128), F32),
-            jax.ShapeDtypeStruct((3, SPAN, 512), F32),
-            jax.ShapeDtypeStruct((3, SPAN, 512), F32),
-        ),
-        in_specs=[vmem] * 8,
+        out_shape=shapes,
+        in_specs=[far] * 8,
         out_specs=(vmem, vmem, vmem),
         scratch_shapes=[
+            pltpu.VMEM((160, 128), F32),
+            pltpu.VMEM((NBLK, BP), jnp.int32),
+            pltpu.VMEM((3, NBLK, BP), F32),
+            pltpu.VMEM((NBLK * BP, 128), BF16),
+            pltpu.VMEM((1, NBLK), jnp.int32),
+            pltpu.VMEM((1, NBLK), jnp.int32),
+            pltpu.VMEM((SPAN, 512), F32),
+            pltpu.VMEM((SPAN, 512), F32),
             pltpu.VMEM((8, 128), jnp.int32),
+            pltpu.VMEM((8, 128), jnp.int32),
+            pltpu.VMEM((3, NBLK, 128), F32),
             pltpu.VMEM((32, 128), F32),
             pltpu.VMEM((NROW, 8, 128), F32),
             pltpu.VMEM((NROW, 8, 128), F32),
-            pltpu.VMEM((SPAN, 16, 128), F32),
-            pltpu.VMEM((NX, 16, 128), F32),
-            pltpu.VMEM((16, 128), F32),
-            pltpu.VMEM((NY, 16, 128), F32),
-            pltpu.VMEM((ROWS, 16, 128), F32),
-            pltpu.VMEM((8, 128), F32),
-            pltpu.VMEM((NROW, 8, 128), F32),
+            pltpu.VMEM((SPAN, LINE, 128), F32),
+            pltpu.VMEM((NX, LINE, 128), F32),
+            pltpu.VMEM((LINE, 128), F32),
+            pltpu.VMEM((NY, LINE, 128), F32),
+            pltpu.VMEM((ROWS, LINE, 128), F32),
+            pltpu.VMEM((1, 128), F32),
+            pltpu.VMEM((NROW, 1, 128), F32),
             pltpu.VMEM((2, 24, 128), F32),
             pltpu.VMEM((5, 8, 128), F32),
             pltpu.VMEM((5, 8, 128), F32),
@@ -502,6 +560,7 @@
             pltpu.VMEM((2, 2, 8, 128), F32),
             pltpu.VMEM((HALO + 1, SPAN, 16, 128), F32),
             pltpu.VMEM((HALO + 1, 3, SPAN, 512), F32),
+            dma((8,)),
             dma((7,)),
             dma((7,)),
             dma((12,)),
@@ -514,7 +573,16 @@
         ),
         cost_estimate=pl.CostEstimate(flops=20_000_000, bytes_accessed=600_000, transcendentals=0),
         name="coupling_step",
-    )(flow, point_cell, normals, rbf_weights, owner, start, stiff_diag, stiff_chord)
+    )(*[pltpu.with_memory_space_constraint(array, pltpu.HBM) for array in arrays])
+    fluid_next, displacement, residual = pl.pallas_call(
+        write_out,
+        out_shape=shapes,
+        in_specs=[vmem] * 3,
+        out_specs=(far, far, far),
+        scratch_shapes=[dma((3,))],
+        compiler_params=pltpu.CompilerParams(vmem_limit_bytes=1024 * 1024),
+        name="write_out",
+    )(*[pltpu.with_memory_space_constraint(result, pltpu.VMEM) for result in results])
     return fluid_next.reshape(5, 4, 8, 128), displacement, residual
 
 

time: 59.9 us -> 50.8 us (0.85)
  local copies, waits for them, and re-layouts: 7.3 us -> 0 us
  Pallas kernels: 51.5 us -> 50 us
    unnamed x15 -> x0, local copies, waits for them, and re-layouts: 5.88 us -> none
    pallas_call x1 -> x2, Pallas kernels: 51.5 us -> 50 us  [the longest x1 49.3 us: per_device(): pl.pallas_call(kernel, out_shape=shapes, in_specs=[far] * 8, out_specs=(v...]
    another operation x2 -> x0, local copies, waits for them, and re-layouts: 0.74 us -> none  [per_device(): owner = jnp.tile(block_owner.reshape(1, NBLK), (1, 3))]
    pad x2 -> x0, local copies, waits for them, and re-layouts: 0.67 us -> none  [the longest x1 0.67 us: per_device(): start = jnp.pad(block_start.reshape(1, NBLK), ((0, 0), (0, 128 - NBLK)))]
where the time goes in v2:
time: 50.8 us; the launch traced here: 50.6 us
  Pallas kernels  50 us (98%)
  between operations  0.64 us (1%)
    pallas_call x1, Pallas kernels, per_device(): pl.pallas_call(kernel, out_shape=shapes, in_specs=[far] * 8, out_specs=(v...  49.3 us

profile of v2, /device:TPU:1, one launch (start us, length us, event | category | flops | bytes accessed | tf_op | source)
XLA Modules:
  0.0 50.6 jit_solution(14337393895305003526)
XLA Ops:
  0.6 49.3 %coupling_step.1 = (f32[160,128]{1,0:T(8,128)S(1)}, f32[3,8,512]{2,1,0:T(8,128)S(1)}, f32[3,8,512]{2,1,0:T(8,128)S(1)}) custom-call(f32[160,128]{1,0:T(8,128)} %bitcast.6, s32[16,64]{1,0:T(8,128)} %cell_far.1, f32[3,16,64]{2,1,0:T(8,128)} %normals_far.1, bf16[1024,128]{1,0:T(8,128)(2,1)} %bitcast.5, s32[1,16]{1,0:T(1,128)} %bitcast.7, s32[1,16]{1,0:T(1,128)} %bitcast.8, ...), custom_call_target="tpu_custom_call" | custom-call | flops 20000000 | bytes 600000 | tf_op jit(solution)/shard_map/coupling_step/pallas_call | solution.py:525
  49.9 0.7 %write_out.1 = (f32[160,128]{1,0:T(8,128)}, f32[3,8,512]{2,1,0:T(8,128)}, f32[3,8,512]{2,1,0:T(8,128)}) custom-call(f32[160,128]{1,0:T(8,128)S(1)} %get-tuple-element.9.fluid, f32[3,8,512]{2,1,0:T(8,128)S(1)} %get-tuple-element.10.displacement, f32[3,8,512]{2,1,0:T(8,128)S(1)} %get-tuple-element.11.residual), custom_call_target="tpu_custom_call" | custom-call | tf_op jit(solution)/shard_map/write_out/pallas_call | solution.py:577

commit v3 on v2

--- a/solution.py
+++ b/solution.py
@@ -249,9 +249,6 @@
     for k in FAR_FIRST:
         greet(x_peer(k), row)
         greet(y_peer(k), row)
-    for k in FAR_FIRST:
-        greet(x_peer(k), row_up)
-        greet(x_peer(k), row_down)
     greet(brick_up, row)
     greet(brick_down, row)
 
@@ -274,7 +271,7 @@
     y_edges[0, 0:20, :] = flow[pl.ds(0, 20, stride=8), :]
     y_edges[1, 0:20, :] = flow[pl.ds(7, 20, stride=8), :]
 
-    pl.semaphore_wait(barrier, (NROW - 1) + 3 * (NX - 1) + (NY - 1) + 2)
+    pl.semaphore_wait(barrier, (NROW - 1) + 1 * (NX - 1) + (NY - 1) + 2)
 
     for k in ROW_FAR_FIRST:
         to = lax.rem(row + k, NROW)

time: 50.8 us -> 49.1 us (0.967)
  Pallas kernels: 50 us -> 48.3 us
    pallas_call x1, Pallas kernels: 49.3 us -> 47.6 us  [per_device(): pl.pallas_call(kernel, out_shape=shapes, in_specs=[far] * 8, out_specs=(v...]
where the time goes in v3:
time: 49.1 us; the launch traced here: 49 us
  Pallas kernels  48.3 us (98%)
  between operations  0.64 us (1%)
    pallas_call x1, Pallas kernels, per_device(): pl.pallas_call(kernel, out_shape=shapes, in_specs=[far] * 8, out_specs=(v...  47.6 us

profile of v3, /device:TPU:1, one launch (start us, length us, event | category | flops | bytes accessed | tf_op | source)
XLA Modules:
  0.0 49.0 jit_solution(10659539183898578534)
XLA Ops:
  0.6 47.6 %coupling_step.1 = (f32[160,128]{1,0:T(8,128)S(1)}, f32[3,8,512]{2,1,0:T(8,128)S(1)}, f32[3,8,512]{2,1,0:T(8,128)S(1)}) custom-call(f32[160,128]{1,0:T(8,128)} %bitcast.6, s32[16,64]{1,0:T(8,128)} %cell_far.1, f32[3,16,64]{2,1,0:T(8,128)} %normals_far.1, bf16[1024,128]{1,0:T(8,128)(2,1)} %bitcast.5, s32[1,16]{1,0:T(1,128)} %bitcast.7, s32[1,16]{1,0:T(1,128)} %bitcast.8, ...), custom_call_target="tpu_custom_call" | custom-call | flops 20000000 | bytes 600000 | tf_op jit(solution)/shard_map/coupling_step/pallas_call | solution.py:522
  48.3 0.7 %write_out.1 = (f32[160,128]{1,0:T(8,128)}, f32[3,8,512]{2,1,0:T(8,128)}, f32[3,8,512]{2,1,0:T(8,128)}) custom-call(f32[160,128]{1,0:T(8,128)S(1)} %get-tuple-element.9.fluid, f32[3,8,512]{2,1,0:T(8,128)S(1)} %get-tuple-element.10.displacement, f32[3,8,512]{2,1,0:T(8,128)S(1)} %get-tuple-element.11.residual), custom_call_target="tpu_custom_call" | custom-call | tf_op jit(solution)/shard_map/write_out/pallas_call | solution.py:574

commit v4 on v3

--- a/solution.py
+++ b/solution.py
@@ -211,7 +211,7 @@
     packed_cell, line_of, doubled, pressure, windows_out, windows_in, dense, x_in, x_sum, y_in, lines,
     shares_out, shares_in, y_edges, x_low, x_high, y_low, y_high,
     diag_rows, chord_rows, diag_halo, chord_halo, fields, turned,
-    load_sem, send_sem, recv_sem, fluid_send, fluid_recv, stiff_send, stiff_recv,
+    reach, load_sem, send_sem, recv_sem, fluid_send, fluid_recv, stiff_send, stiff_recv,
 ):
     brick = lax.axis_index("brick")
     row = lax.axis_index("row")
@@ -246,11 +246,9 @@
     for load in loads:
         load.start()
 
-    for k in FAR_FIRST:
-        greet(x_peer(k), row)
-        greet(y_peer(k), row)
-    greet(brick_up, row)
-    greet(brick_down, row)
+    near = ((x_peer(1), row), (x_peer(NX - 1), row), (y_peer(1), row), (y_peer(NY - 1), row))
+    for to in near + ((brick_up, row), (brick_down, row)):
+        greet(*to)
 
     def copy_to(source, target, send, receive, to_brick, to_row):
         return pltpu.make_async_remote_copy(
@@ -271,13 +269,19 @@
     y_edges[0, 0:20, :] = flow[pl.ds(0, 20, stride=8), :]
     y_edges[1, 0:20, :] = flow[pl.ds(7, 20, stride=8), :]
 
-    pl.semaphore_wait(barrier, (NROW - 1) + 1 * (NX - 1) + (NY - 1) + 2)
+    pl.semaphore_wait(barrier, (NROW - 1) + 6)
+
+    def tell(semaphore, to):
+        pl.semaphore_signal(semaphore, inc=1, device_id=to, device_id_type=MESH)
 
     for k in ROW_FAR_FIRST:
         to = lax.rem(row + k, NROW)
         copy_to(windows_out.at[to], windows_in.at[row], send_sem.at[0], recv_sem.at[0], brick, to).start()
 
     windows_in[row] = windows_out[row]
+
+    for n, to in enumerate(near):
+        tell(reach.at[n // 2], to)
 
     fluid_copies = [
         copy_to(y_edges.at[0], y_high, fluid_send.at[0], fluid_recv.at[0], brick, row_down),
@@ -309,12 +313,19 @@
     for copy in stiff_copies:
         copy.start()
 
+    for axis in range(2):
+        pl.semaphore_wait(reach.at[axis], 2)
+    for n, to in enumerate(((x_peer(2), row), (x_peer(NX - 2), row), (y_peer(2), row), (y_peer(NY - 2), row))):
+        tell(reach.at[2 + n // 2], to)
+
     def await_copies(buffer, count, n):
         part = buffer.at[pl.ds(0, count)]
         copy_to(part, part, send_sem.at[n], recv_sem.at[n], brick_up, row).wait_recv()
 
     await_copies(windows_in, NROW - 1, 0)
     add_windows(windows_in, dense)
+
+    pl.semaphore_wait(reach.at[2], 2)
 
     for k in FAR_FIRST:
         to = lax.rem(x + k, NX)
@@ -326,6 +337,8 @@
     for k in range(1, NX):
         total = total + x_in[k]
     x_sum[...] = total
+
+    pl.semaphore_wait(reach.at[3], 2)
 
     for k in FAR_FIRST:
         copy_to(x_sum, y_in.at[y], send_sem.at[2], recv_sem.at[2], y_peer(k), row).start()
@@ -557,6 +570,7 @@
             pltpu.VMEM((2, 2, 8, 128), F32),
             pltpu.VMEM((HALO + 1, SPAN, 16, 128), F32),
             pltpu.VMEM((HALO + 1, 3, SPAN, 512), F32),
+            pltpu.SemaphoreType.REGULAR((4,)),
             dma((8,)),
             dma((7,)),
             dma((7,)),

time: 49.1 us -> 48.1 us (0.980)
  Pallas kernels: 48.3 us -> 47.3 us
    pallas_call x1, Pallas kernels: 47.6 us -> 46.6 us  [per_device(): pl.pallas_call(kernel, out_shape=shapes, in_specs=[far] * 8, out_specs=(v...]
where the time goes in v4:
time: 48.1 us; the launch traced here: 48 us
  Pallas kernels  47.3 us (98%)
  between operations  0.64 us (1%)
    pallas_call x1, Pallas kernels, per_device(): pl.pallas_call(kernel, out_shape=shapes, in_specs=[far] * 8, out_specs=(v...  46.6 us

profile of v4, /device:TPU:1, one launch (start us, length us, event | category | flops | bytes accessed | tf_op | source)
XLA Modules:
  0.0 48.0 jit_solution(11369417530176764742)
XLA Ops:
  0.6 46.6 %coupling_step.1 = (f32[160,128]{1,0:T(8,128)S(1)}, f32[3,8,512]{2,1,0:T(8,128)S(1)}, f32[3,8,512]{2,1,0:T(8,128)S(1)}) custom-call(f32[160,128]{1,0:T(8,128)} %bitcast.6, s32[16,64]{1,0:T(8,128)} %cell_far.1, f32[3,16,64]{2,1,0:T(8,128)} %normals_far.1, bf16[1024,128]{1,0:T(8,128)(2,1)} %bitcast.5, s32[1,16]{1,0:T(1,128)} %bitcast.7, s32[1,16]{1,0:T(1,128)} %bitcast.8, ...), custom_call_target="tpu_custom_call" | custom-call | flops 20000000 | bytes 600000 | tf_op jit(solution)/shard_map/coupling_step/pallas_call | solution.py:535
  47.3 0.7 %write_out.1 = (f32[160,128]{1,0:T(8,128)}, f32[3,8,512]{2,1,0:T(8,128)}, f32[3,8,512]{2,1,0:T(8,128)}) custom-call(f32[160,128]{1,0:T(8,128)S(1)} %get-tuple-element.9.fluid, f32[3,8,512]{2,1,0:T(8,128)S(1)} %get-tuple-element.10.displacement, f32[3,8,512]{2,1,0:T(8,128)S(1)} %get-tuple-element.11.residual), custom_call_target="tpu_custom_call" | custom-call | tf_op jit(solution)/shard_map/write_out/pallas_call | solution.py:588

commit v5 on v4

--- a/solution.py
+++ b/solution.py
@@ -210,7 +210,7 @@
     flow, cell, normals, weights, owner, start, stiff_diag, stiff_chord,
     packed_cell, line_of, doubled, pressure, windows_out, windows_in, dense, x_in, x_sum, y_in, lines,
     shares_out, shares_in, y_edges, x_low, x_high, y_low, y_high,
-    diag_rows, chord_rows, diag_halo, chord_halo, fields, turned,
+    diag_rows, chord_rows, diag_halo, chord_halo, factors, fields, turned,
     reach, load_sem, send_sem, recv_sem, fluid_send, fluid_recv, stiff_send, stiff_recv,
 ):
     brick = lax.axis_index("brick")
@@ -274,14 +274,19 @@
     def tell(semaphore, to):
         pl.semaphore_signal(semaphore, inc=1, device_id=to, device_id_type=MESH)
 
+    for n, to in enumerate(near):
+        tell(reach.at[n // 2], to)
+
     for k in ROW_FAR_FIRST:
         to = lax.rem(row + k, NROW)
         copy_to(windows_out.at[to], windows_in.at[row], send_sem.at[0], recv_sem.at[0], brick, to).start()
 
     windows_in[row] = windows_out[row]
 
-    for n, to in enumerate(near):
-        tell(reach.at[n // 2], to)
+    for axis in range(2):
+        pl.semaphore_wait(reach.at[axis], 2)
+    for n, to in enumerate(((x_peer(2), row), (x_peer(NX - 2), row), (y_peer(2), row), (y_peer(NY - 2), row))):
+        tell(reach.at[2 + n // 2], to)
 
     fluid_copies = [
         copy_to(y_edges.at[0], y_high, fluid_send.at[0], fluid_recv.at[0], brick, row_down),
@@ -313,11 +318,6 @@
     for copy in stiff_copies:
         copy.start()
 
-    for axis in range(2):
-        pl.semaphore_wait(reach.at[axis], 2)
-    for n, to in enumerate(((x_peer(2), row), (x_peer(NX - 2), row), (y_peer(2), row), (y_peer(NY - 2), row))):
-        tell(reach.at[2 + n // 2], to)
-
     def await_copies(buffer, count, n):
         part = buffer.at[pl.ds(0, count)]
         copy_to(part, part, send_sem.at[n], recv_sem.at[n], brick_up, row).wait_recv()
@@ -350,6 +350,17 @@
     fluid_step(flow, x_low, x_high, y_low, y_high, fluid_next)
     for copy in stiff_copies:
         copy.wait_recv()
+    for i in range(1, ROWS - 1):
+        if i < HALO:
+            own_diag, own_chord = diag_halo[0, i - 1], chord_halo[0, i - 1]
+        elif i < HALO + SPAN:
+            own_diag, own_chord = diag_rows[i - HALO], chord_rows[i - HALO]
+        else:
+            own_diag, own_chord = diag_halo[1, i - HALO - SPAN], chord_halo[1, i - HALO - SPAN]
+        chord_before = node_before(own_chord)
+        factors[0, i] = (own_diag + (2.0 - CENTRE) + (own_chord + chord_before)) * (1.0 / WIDTH)
+        factors[1, i] = own_chord * (1.0 / WIDTH)
+        factors[2, i] = chord_before * (1.0 / WIDTH)
 
     await_copies(y_in, NY - 1, 2)
     total = y_in[0]
@@ -400,12 +411,6 @@
 
     below = jnp.where(row > 0, 1.0, 0.0).astype(F32)
     above = jnp.where(row < NROW - 1, 1.0, 0.0).astype(F32)
-    diag = [None, diag_halo[0, 0], diag_halo[0, 1]] + [diag_rows[s] for s in range(SPAN)]
-    diag = diag + [diag_halo[1, 0], diag_halo[1, 1]]
-    chord = [None, chord_halo[0, 0], chord_halo[0, 1]] + [chord_rows[s] for s in range(SPAN)]
-    chord = chord + [chord_halo[1, 0], chord_halo[1, 1]]
-    diag = [None if d is None else (d + (2.0 - CENTRE)) * (1.0 / WIDTH) for d in diag]
-    chord = [None if d is None else d * (1.0 / WIDTH) for d in chord]
     products = [jnp.zeros((8, 128), F32) for _ in range(6)]
     for half in range(2):
         part = slice(8 * half, 8 * half + 8)
@@ -418,9 +423,9 @@
             before = levels[-1]
             after = [None] * ROWS
             for i in range(level, ROWS - level):
-                flow_on = chord[i] * (before[i] - next_node(before[i]))
-                value = diag[i] * before[i] + (flow_on - node_before(flow_on))
-                value = value - (1.0 / WIDTH) * (before[i - 1] + before[i + 1])
+                sides = (1.0 / WIDTH) * (before[i - 1] + before[i + 1])
+                around = factors[1, i] * next_node(before[i]) + factors[2, i] * node_before(before[i])
+                value = factors[0, i] * before[i] - sides - around
                 if i < HALO:
                     value = value * below
                 if i >= HALO + SPAN:
@@ -568,6 +573,7 @@
             pltpu.VMEM((SPAN, 8, 128), F32),
             pltpu.VMEM((2, 2, 8, 128), F32),
             pltpu.VMEM((2, 2, 8, 128), F32),
+            pltpu.VMEM((3, ROWS, 8, 128), F32),
             pltpu.VMEM((HALO + 1, SPAN, 16, 128), F32),
             pltpu.VMEM((HALO + 1, 3, SPAN, 512), F32),
             pltpu.SemaphoreType.REGULAR((4,)),

time: 48.1 us -> 47.8 us (level)
  no operation moved by 1% of the time
where the time goes in v5:
time: 47.8 us; the launch traced here: 47.7 us
  Pallas kernels  47 us (98%)
  between operations  0.64 us (1%)
    pallas_call x1, Pallas kernels, per_device(): pl.pallas_call(kernel, out_shape=shapes, in_specs=[far] * 8, out_specs=(v...  46.3 us

profile of v5, /device:TPU:1, one launch (start us, length us, event | category | flops | bytes accessed | tf_op | source)
XLA Modules:
  0.0 47.7 jit_solution(12004014751579016812)
XLA Ops:
  0.6 46.3 %coupling_step.1 = (f32[160,128]{1,0:T(8,128)S(1)}, f32[3,8,512]{2,1,0:T(8,128)S(1)}, f32[3,8,512]{2,1,0:T(8,128)S(1)}) custom-call(f32[160,128]{1,0:T(8,128)} %bitcast.6, s32[16,64]{1,0:T(8,128)} %cell_far.1, f32[3,16,64]{2,1,0:T(8,128)} %normals_far.1, bf16[1024,128]{1,0:T(8,128)(2,1)} %bitcast.5, s32[1,16]{1,0:T(1,128)} %bitcast.7, s32[1,16]{1,0:T(1,128)} %bitcast.8, ...), custom_call_target="tpu_custom_call" | custom-call | flops 20000000 | bytes 600000 | tf_op jit(solution)/shard_map/coupling_step/pallas_call | solution.py:540
  47.0 0.7 %write_out.1 = (f32[160,128]{1,0:T(8,128)}, f32[3,8,512]{2,1,0:T(8,128)}, f32[3,8,512]{2,1,0:T(8,128)}) custom-call(f32[160,128]{1,0:T(8,128)S(1)} %get-tuple-element.9.fluid, f32[3,8,512]{2,1,0:T(8,128)S(1)} %get-tuple-element.10.displacement, f32[3,8,512]{2,1,0:T(8,128)S(1)} %get-tuple-element.11.residual), custom_call_target="tpu_custom_call" | custom-call | tf_op jit(solution)/shard_map/write_out/pallas_call | solution.py:594

commit v6 on v5

--- a/solution.py
+++ b/solution.py
@@ -412,6 +412,7 @@
     below = jnp.where(row > 0, 1.0, 0.0).astype(F32)
     above = jnp.where(row < NROW - 1, 1.0, 0.0).astype(F32)
     products = [jnp.zeros((8, 128), F32) for _ in range(6)]
+    kept = []
     for half in range(2):
         part = slice(8 * half, 8 * half + 8)
         if half == 0:
@@ -434,7 +435,7 @@
             levels.append(after)
         for i in range(HALO, HALO + SPAN):
             for level in range(HALO + 1):
-                fields[level, i - HALO, part, :] = levels[level][i]
+                kept.append((level, i - HALO, part, levels[level][i]))
             for n, (p, q) in enumerate(((0, 0), (0, 1), (1, 1), (1, 2), (2, 2), (2, 3))):
                 products[n] = products[n] + levels[p][i] * levels[q][i]
     share = jnp.zeros((1, 128), F32)
@@ -450,6 +451,8 @@
 
     shares_in[row] = shares_out[...]
 
+    for level, s, part, value in kept:
+        fields[level, s, part, :] = value
     for level in range(HALO + 1):
         for s in range(SPAN):
             for c in range(3):

time: 47.8 us -> 47.8 us (level)
  no operation moved by 1% of the time
where the time goes in v6:
time: 47.8 us; the launch traced here: 47.7 us
  Pallas kernels  47 us (98%)
  between operations  0.64 us (1%)
    pallas_call x1, Pallas kernels, per_device(): pl.pallas_call(kernel, out_shape=shapes, in_specs=[far] * 8, out_specs=(v...  46.3 us

profile of v6, /device:TPU:1, one launch (start us, length us, event | category | flops | bytes accessed | tf_op | source)
XLA Modules:
  0.0 47.7 jit_solution(18033776796005009377)
XLA Ops:
  0.6 46.3 %coupling_step.1 = (f32[160,128]{1,0:T(8,128)S(1)}, f32[3,8,512]{2,1,0:T(8,128)S(1)}, f32[3,8,512]{2,1,0:T(8,128)S(1)}) custom-call(f32[160,128]{1,0:T(8,128)} %bitcast.6, s32[16,64]{1,0:T(8,128)} %cell_far.1, f32[3,16,64]{2,1,0:T(8,128)} %normals_far.1, bf16[1024,128]{1,0:T(8,128)(2,1)} %bitcast.5, s32[1,16]{1,0:T(1,128)} %bitcast.7, s32[1,16]{1,0:T(1,128)} %bitcast.8, ...), custom_call_target="tpu_custom_call" | custom-call | flops 20000000 | bytes 600000 | tf_op jit(solution)/shard_map/coupling_step/pallas_call | solution.py:543
  47.0 0.7 %write_out.1 = (f32[160,128]{1,0:T(8,128)}, f32[3,8,512]{2,1,0:T(8,128)}, f32[3,8,512]{2,1,0:T(8,128)}) custom-call(f32[160,128]{1,0:T(8,128)S(1)} %get-tuple-element.9.fluid, f32[3,8,512]{2,1,0:T(8,128)S(1)} %get-tuple-element.10.displacement, f32[3,8,512]{2,1,0:T(8,128)S(1)} %get-tuple-element.11.residual), custom_call_target="tpu_custom_call" | custom-call | tf_op jit(solution)/shard_map/write_out/pallas_call | solution.py:597
